TPU v7x, 256 devices: a whole 4x4x8 slice. The times are simulated.
256 devices in a mesh: expert: 32 (over y, x, core), rep: 8 (over z).
Axes of the slice: x: 4, y: 4, z: 8, core: 2. Of those that a mesh axis runs over, the one named last changes fastest.
Arguments:
- node_feats: bfloat16 [8, 8192, 768], P('rep', 'expert'), may hold values from -32 to 32
- edge_src: int32 [8, 32768], P('rep', 'expert'), may hold values from 0 to 383, as said below
- edge_dst: int32 [8, 32768], P('rep', 'expert'), may hold values from -1 to 255, as said below
- node_codes: int32 [8, 8192, 1], P('rep', 'expert'), may hold values from 0 to 31, as said below
- norm_gain: float32 [768], replicated, may hold values from 0.1 to 1.9
- w_gate: bfloat16 [32, 768, 1536], P('expert'), may hold values from -0.21875 to 0.21875
- w_up: bfloat16 [32, 768, 1536], P('expert'), may hold values from -0.21875 to 0.21875
- w_down_t: bfloat16 [32, 768, 1536], P('expert'), may hold values from -0.15625 to 0.15625
- d_out: bfloat16 [8, 8192, 768], P('rep', 'expert'), may hold values from -6 to 6
Outputs:
- layer_out: bfloat16 [8, 8192, 768], P('rep', 'expert')
- d_node_feats: bfloat16 [8, 8192, 768], P('rep', 'expert')
- grad_w_gate: float32 [32, 768, 1536], P('expert', None, 'rep')
- grad_w_up: float32 [32, 768, 1536], P('expert', None, 'rep')
- grad_w_down_t: float32 [32, 768, 1536], P('expert', None, 'rep')
Inputs may be any that keep to these rules, and one draw needn't show every extreme that they name: `node_codes`: within each partition (256 consecutive nodes of a graph) at most 16 nodes carry one code; one code, the same for all partitions of a draw, is carried by exactly 16 nodes of every partition. `edge_src`: A row of the partition's extended rows: the last 64 nodes of the previous partition, then its own 256 nodes, then the first 64 nodes of the next partition. `edge_dst`: A node's position within the partition, or -1 for a padding slot; a partition's padding slots are the last of its 1024 slots, at least one.
All inputs are finite; a program needn't handle non-finite values.
Results may differ from a plain program's by a relative error of at most 0.015.
Values may be sent and summed in bfloat16 or wider, within the bound.
A program may use at most 128 MiB of HBM per device.

v0:
```python
import jax
import jax.numpy as jnp
from jax import lax
from jax.sharding import PartitionSpec as P


def extended_2(array, sides, width):
    for axis, dim in sides:
        count, length = (lax.axis_size(axis), array.shape[dim])
        up = [(i, (i + 1) % count) for i in range(count)]
        down = [(j, i) for i, j in up]
        last = lax.slice_in_dim(array, length - width, length, axis=dim)
        first = lax.slice_in_dim(array, 0, width, axis=dim)
        before = lax.ppermute(last, axis, up)
        after = lax.ppermute(first, axis, down)
        array = jnp.concatenate([before, array, after], axis=dim)
    return array


def contract_rows(left, right):
    return lax.dot_general(
        left, right, (((0,), (0,)), ((), ())), preferred_element_type=jnp.float32
    )


def contract_last(left, right):
    return lax.dot_general(
        left, right, (((1,), (1,)), ((), ())), preferred_element_type=jnp.float32
    )


def on_device(node_feats, edge_src, edge_dst, node_codes, norm_gain, w_gate, w_up, w_down_t, d_out):
    node_count = node_feats.shape[1]
    width = node_feats.shape[2]
    expert_count = lax.axis_size("expert")
    capacity = 2 * node_count // expert_count
    rim_width = node_count // 4
    own_rows = node_feats[0].astype(jnp.float32)
    extended = extended_2(node_feats, (("expert", 1),), rim_width)[0]
    extent = extended.shape[0]
    sources = edge_src[0]
    targets = edge_dst[0]
    source_hot = (sources[:, None] == jnp.arange(extent, dtype=jnp.int32)[None, :]).astype(
        jnp.bfloat16
    )
    source_hot_t = (jnp.arange(extent, dtype=jnp.int32)[:, None] == sources[None, :]).astype(
        jnp.bfloat16
    )
    target_hot = (targets[:, None] == jnp.arange(node_count, dtype=jnp.int32)[None, :]).astype(
        jnp.bfloat16
    )
    target_hot_t = (jnp.arange(node_count, dtype=jnp.int32)[:, None] == targets[None, :]).astype(
        jnp.bfloat16
    )
    message = jnp.dot(source_hot, extended, preferred_element_type=jnp.float32).astype(jnp.bfloat16)
    summed = jnp.dot(target_hot_t, message, preferred_element_type=jnp.float32)
    degree = jnp.sum(target_hot_t, axis=1, dtype=jnp.float32)
    inverse = 1.0 / jnp.maximum(degree, 1.0)
    mixed_rows = own_rows + summed * inverse[:, None]
    scaling = lax.rsqrt(jnp.mean(mixed_rows * mixed_rows, axis=1, keepdims=True) + 1e-05)
    normal = mixed_rows * scaling
    routed = (normal * norm_gain[None, :]).astype(jnp.bfloat16)
    expert_ids = node_codes[0, :, 0]
    member = (expert_ids[:, None] == jnp.arange(expert_count, dtype=jnp.int32)[None, :]).astype(
        jnp.int32
    )
    slot_ids = jnp.sum((jnp.cumsum(member, axis=0) - member) * member, axis=1)
    row_count = expert_count * capacity
    slot_flat = expert_ids * capacity + slot_ids
    placement = (slot_flat[:, None] == jnp.arange(row_count, dtype=jnp.int32)[None, :]).astype(
        jnp.bfloat16
    )
    placement_t = (jnp.arange(row_count, dtype=jnp.int32)[:, None] == slot_flat[None, :]).astype(
        jnp.bfloat16
    )
    outgoing = jnp.concatenate([routed, d_out[0]], 1)
    bucketed = jnp.dot(placement_t, outgoing, preferred_element_type=jnp.float32).astype(
        jnp.bfloat16
    )
    send_rows = bucketed[:, :width].reshape(expert_count, capacity, width)
    send_grads = bucketed[:, width:].reshape(expert_count, capacity, width)
    recv_rows, recv_grads = (
        lax.all_to_all(send_rows, "expert", split_axis=0, concat_axis=0, tiled=True),
        lax.all_to_all(send_grads, "expert", split_axis=0, concat_axis=0, tiled=True),
    )
    rows_in = recv_rows.reshape(row_count, width)
    grads_in = recv_grads.reshape(row_count, width)
    gate_weight = w_gate[0]
    up_weight = w_up[0]
    down_weight = w_down_t[0]
    gate_pre = jnp.dot(rows_in, gate_weight, preferred_element_type=jnp.float32)
    up_pre = jnp.dot(rows_in, up_weight, preferred_element_type=jnp.float32)
    sigmoid_gate = jax.nn.sigmoid(gate_pre)
    silu_gate = gate_pre * sigmoid_gate
    hidden = (silu_gate * up_pre).astype(jnp.bfloat16)
    expert_out = contract_last(hidden, down_weight).astype(jnp.bfloat16)
    back_hidden = jnp.dot(grads_in, down_weight, preferred_element_type=jnp.float32)
    d_gate = (back_hidden * up_pre * sigmoid_gate * (1.0 + gate_pre * (1.0 - sigmoid_gate))).astype(
        jnp.bfloat16
    )
    d_up = (back_hidden * silu_gate).astype(jnp.bfloat16)
    d_rows = (contract_last(d_gate, gate_weight) + contract_last(d_up, up_weight)).astype(
        jnp.bfloat16
    )
    returned, d_returned = (
        lax.all_to_all(
            expert_out.reshape(expert_count, capacity, width),
            "expert",
            split_axis=0,
            concat_axis=0,
            tiled=True,
        ),
        lax.all_to_all(
            d_rows.reshape(expert_count, capacity, width),
            "expert",
            split_axis=0,
            concat_axis=0,
            tiled=True,
        ),
    )
    incoming = jnp.concatenate(
        [returned.reshape(row_count, width), d_returned.reshape(row_count, width)], 1
    )
    collected = jnp.dot(placement, incoming, preferred_element_type=jnp.float32)
    node_out = collected[:, :width]
    d_routed = collected[:, width:]
    layer_out = (own_rows + node_out).astype(jnp.bfloat16)
    grad_gate, grad_up, grad_down = (
        lax.psum_scatter(
            contract_rows(rows_in, d_gate)[None].astype(jnp.bfloat16),
            "rep",
            scatter_dimension=2,
            tiled=True,
        ).astype(jnp.float32),
        lax.psum_scatter(
            contract_rows(rows_in, d_up)[None].astype(jnp.bfloat16),
            "rep",
            scatter_dimension=2,
            tiled=True,
        ).astype(jnp.float32),
        lax.psum_scatter(
            contract_rows(grads_in, hidden)[None].astype(jnp.bfloat16),
            "rep",
            scatter_dimension=2,
            tiled=True,
        ).astype(jnp.float32),
    )
    d_norm = d_routed * norm_gain[None, :]
    d_mixed = scaling * (d_norm - normal * jnp.mean(d_norm * normal, axis=1, keepdims=True))
    d_mean = (d_mixed * inverse[:, None]).astype(jnp.bfloat16)
    d_message = jnp.dot(target_hot, d_mean, preferred_element_type=jnp.float32).astype(jnp.bfloat16)
    d_extended = jnp.dot(source_hot_t, d_message, preferred_element_type=jnp.float32)
    outer_rows = jnp.concatenate([d_extended[:rim_width], d_extended[rim_width + node_count :]], 0)
    arrived = extended_2(outer_rows[None].astype(jnp.bfloat16), (("expert", 1),), rim_width).astype(
        jnp.float32
    )[0]
    inner = d_extended[rim_width : rim_width + node_count]
    inner = inner.at[:rim_width].add(arrived[:rim_width])
    inner = inner.at[node_count - rim_width :].add(arrived[3 * rim_width :])
    d_node = (d_out[0].astype(jnp.float32) + d_mixed + inner).astype(jnp.bfloat16)
    return (layer_out[None], d_node[None], grad_gate, grad_up, grad_down)


def solution(mesh):
    return jax.shard_map(
        on_device,
        mesh=mesh,
        in_specs=(
            P("rep", "expert", None),
            P("rep", "expert"),
            P("rep", "expert"),
            P("rep", "expert", None),
            P(),
            P("expert", None, None),
            P("expert", None, None),
            P("expert", None, None),
            P("rep", "expert", None),
        ),
        out_specs=(
            P("rep", "expert", None),
            P("rep", "expert", None),
            P("expert", None, "rep"),
            P("expert", None, "rep"),
            P("expert", None, "rep"),
        ),
        check_vma=False,
    )
```

profile of v0, /device:TPU:4, one launch (start us, length us, event | category | flops | bytes accessed | tf_op | source)
XLA Modules:
  0.0 230.0 jit_solution(13066189525919764098)
XLA Ops:
  15.2 2.8 %multiply_reduce_fusion.1 = (f32[256]{0:T(256)S(1)}, f32[256,768]{1,0:T(8,128)S(1)}) fusion(f32[256]{0:T(256)S(1)} %maximum_divide_fusion, s32[1024]{0:T(1024)} %bitcast.140, bf16[1,64,768]{2,1,0:T(8,128)(2,1)} %copy-done.12, bf16[1,256,768]{2,1,0:T(8,128)(2,1)} %param.13, bf16[1,64,768]{2,1,0:T(8,128)(2,1)} %copy-done.11, s32[1024]{0:T(1024)} %bitcast.138), kind=kOutput, calls=%fused_computation.57 | convolution fusion | flops 1010827008 | bytes 1386496 | tf_op jit(solution)/shard_map/dot_general | solution.py:56
  19.8 22.3 %all_to_all.20 = bf16[32,16,768]{2,1,0:T(8,128)(2,1)} all-to-all(bf16[32,16,768]{2,1,0:T(8,128)(2,1)S(1)} %bitcast.123), channel_id=1, replica_groups=mesh['expert'=32,'rep'=8] {'expert'}, dimensions={0} | all-to-all | bytes 1572864 | tf_op jit(solution)/shard_map/all_to_all | solution.py:83
  42.1 6.5 %all-to-all-start.2 = ((bf16[32,16,768]{2,1,0:T(8,128)(2,1)}), bf16[32,16,768]{2,1,0:T(8,128)(2,1)}, u32[]{:S(2)}, u32[]{:S(2)}) async-start(bf16[32,16,768]{2,1,0:T(8,128)(2,1)} %bitcast.122), calls=%async_computation.2 | async-start | bytes 1572864 | tf_op jit(solution)/shard_map/all_to_all | solution.py:84
  48.7 4.9 %fusion.14 = f32[512,1536]{1,0:T(8,128)} fusion(bf16[512,768]{1,0:T(8,128)(2,1)} %bitcast.125, bf16[1,768,1536]{2,1,0:T(8,128)(2,1)} %param.18), kind=kOutput, calls=%fused_computation.25 | convolution fusion | flops 1207959552 | bytes 6291456 | tf_op jit(solution)/shard_map/dot_general | solution.py:91
  53.6 7.6 %all-to-all-done.2 = bf16[32,16,768]{2,1,0:T(8,128)(2,1)} async-done(((bf16[32,16,768]{2,1,0:T(8,128)(2,1)}), bf16[32,16,768]{2,1,0:T(8,128)(2,1)}, u32[]{:S(2)}, u32[]{:S(2)}) %all-to-all-start.2) | async-done | bytes 786464 | tf_op jit(solution)/shard_map/all_to_all | solution.py:84
  61.3 3.4 %fusion.4 = f32[512,1536]{1,0:T(8,128)S(1)} fusion(bf16[512,768]{1,0:T(8,128)(2,1)} %bitcast.17, bf16[1,768,1536]{2,1,0:T(8,128)(2,1)} %param.20), kind=kOutput, calls=%fused_computation.15 | convolution fusion | flops 1207959552 | bytes 6291456 | tf_op jit(solution)/shard_map/dot_general | solution.py:97
  64.7 3.8 %multiply_convert_fusion.2 = (bf16[512,1536]{1,0:T(8,128)(2,1)}, bf16[512,1536]{1,0:T(8,128)(2,1)}, bf16[512,1536]{1,0:T(8,128)(2,1)S(1)}) fusion(f32[512,1536]{1,0:T(8,128)S(1)} %copy-done.13, f32[512,1536]{1,0:T(8,128)S(1)} %fusion.4, bf16[512,768]{1,0:T(8,128)(2,1)S(1)} %bitcast.127, bf16[1,768,1536]{2,1,0:T(8,128)(2,1)S(1)} %copy-done), kind=kOutput, calls=%fused_computation.5 | convolution fusion | flops 1219756032 | bytes 14155776 | tf_op jit(solution)/shard_map/dot_general | solution.py:92
  69.8 2.8 %fusion.2 = bf16[1,768,1536]{2,1,0:T(8,128)(2,1)} fusion(bf16[512,768]{1,0:T(8,128)(2,1)S(1)} %bitcast.128, bf16[512,1536]{1,0:T(8,128)(2,1)S(1)} %get-tuple-element.51), kind=kOutput, calls=%fused_computation.9 | convolution fusion | flops 1209139200 | bytes 4718592 | tf_op jit(solution)/shard_map/dot_general | solution.py:21
  72.6 12.1 %copy.31 = bf16[1,768,1536]{1,0,2:T(2,128)(2,1)} copy(bf16[1,768,1536]{2,1,0:T(8,128)(2,1)} %fusion.2) | data formatting | bytes 4718592
  84.7 4.2 %copy.44 = bf16[1536,1,768]{2,0,1:T(8,128)(2,1)} copy(bf16[1536,1,768]{2,1,0:T(2,128)(2,1)} %bitcast.116) | data formatting | bytes 4718592
  88.9 4.5 %fusion.1 = bf16[1,768,1536]{2,1,0:T(8,128)(2,1)} fusion(bf16[512,768]{1,0:T(8,128)(2,1)} %bitcast.126, bf16[512,1536]{1,0:T(8,128)(2,1)} %get-tuple-element.50), kind=kOutput, calls=%fused_computation.8 | convolution fusion | flops 1209139200 | bytes 4718592 | tf_op jit(solution)/shard_map/dot_general | solution.py:21
  93.5 12.1 %copy.29 = bf16[1,768,1536]{1,0,2:T(2,128)(2,1)} copy(bf16[1,768,1536]{2,1,0:T(8,128)(2,1)} %fusion.1) | data formatting | bytes 4718592
  105.5 4.3 %copy.45 = bf16[1536,1,768]{2,0,1:T(8,128)(2,1)} copy(bf16[1536,1,768]{2,1,0:T(2,128)(2,1)} %bitcast.117) | data formatting | bytes 4718592
  110.1 4.5 %fusion.3 = bf16[1,768,1536]{2,1,0:T(8,128)(2,1)} fusion(bf16[512,768]{1,0:T(8,128)(2,1)} %bitcast.17, bf16[512,1536]{1,0:T(8,128)(2,1)} %get-tuple-element.49), kind=kOutput, calls=%fused_computation.10 | convolution fusion | flops 1209139200 | bytes 4718592 | tf_op jit(solution)/shard_map/dot_general | solution.py:21
  114.5 12.1 %copy.33 = bf16[1,768,1536]{1,0,2:T(2,128)(2,1)} copy(bf16[1,768,1536]{2,1,0:T(8,128)(2,1)} %fusion.3) | data formatting | bytes 4718592
  126.7 4.1 %copy.43 = bf16[1536,1,768]{2,0,1:T(8,128)(2,1)} copy(bf16[1536,1,768]{2,1,0:T(2,128)(2,1)} %bitcast.118) | data formatting | bytes 4718592
  130.8 4.5 %fusion.24 = bf16[512,768]{1,0:T(8,128)(2,1)} fusion(bf16[512,1536]{1,0:T(8,128)(2,1)} %get-tuple-element.49, bf16[1,768,1536]{2,1,0:T(8,128)(2,1)} %param.20), kind=kOutput, calls=%fused_computation.38 | convolution fusion | flops 1208352768 | bytes 4718592 | tf_op jit(solution)/shard_map/dot_general | solution.py:27
  135.3 6.5 %all-to-all-start.1 = ((bf16[32,16,768]{2,1,0:T(8,128)(2,1)}), bf16[32,16,768]{2,1,0:T(8,128)(2,1)}, u32[]{:S(2)}, u32[]{:S(2)}) async-start(bf16[32,16,768]{2,1,0:T(8,128)(2,1)} %bitcast.129), calls=%async_computation.1 | async-start | bytes 1572864 | tf_op jit(solution)/shard_map/all_to_all | solution.py:106
  141.8 3.0 %fusion.8 = f32[512,768]{1,0:T(8,128)S(1)} fusion(bf16[512,1536]{1,0:T(8,128)(2,1)} %copy-done.14, bf16[1,768,1536]{2,1,0:T(8,128)(2,1)S(1)} %copy-done), kind=kOutput, calls=%fused_computation.19 | convolution fusion | flops 1207959552 | bytes 5505024 | tf_op jit(solution)/shard_map/dot_general | solution.py:27
  144.8 2.3 %add_convert_fusion = bf16[512,768]{1,0:T(8,128)(2,1)} fusion(f32[512,768]{1,0:T(8,128)S(1)} %fusion.8, bf16[512,1536]{1,0:T(8,128)(2,1)S(1)} %copy-done.15, bf16[1,768,1536]{2,1,0:T(8,128)(2,1)S(1)} %copy-done.10), kind=kOutput, calls=%fused_computation.34 | convolution fusion | flops 1208745984 | bytes 6291456 | tf_op jit(solution)/shard_map/dot_general | solution.py:27
  147.1 7.3 %all-to-all-done.1 = bf16[32,16,768]{2,1,0:T(8,128)(2,1)} async-done(((bf16[32,16,768]{2,1,0:T(8,128)(2,1)}), bf16[32,16,768]{2,1,0:T(8,128)(2,1)}, u32[]{:S(2)}, u32[]{:S(2)}) %all-to-all-start.1) | async-done | bytes 786464 | tf_op jit(solution)/shard_map/all_to_all | solution.py:106
  154.4 18.5 %all_to_all.21 = bf16[32,16,768]{2,1,0:T(8,128)(2,1)S(1)} all-to-all(bf16[32,16,768]{2,1,0:T(8,128)(2,1)} %bitcast.130), channel_id=1, replica_groups=mesh['expert'=32,'rep'=8] {'expert'}, dimensions={0} | all-to-all | bytes 1572864 | tf_op jit(solution)/shard_map/all_to_all | solution.py:113
  176.5 3.5 %fusion.20 = f32[384,768]{1,0:T(8,128)} fusion(s32[1024]{0:T(1024)} %bitcast.141, s32[1024]{0:T(1024)S(1)} %bitcast.139, f32[256]{0:T(256)} %copy-done.9, f32[256,1536]{1,0:T(8,128)} %copy-done.2, f32[256,768]{1,0:T(8,128)S(1)} %get-tuple-element.61, f32[256]{0:T(256)S(1)} %broadcast_multiply_fusion, f32[768]{0:T(1024)S(1)} %copy-done.7, ...), kind=kOutput, calls=%fused_computation.36 | convolution fusion | flops 1009451008 | bytes 2766848 | tf_op jit(solution)/shard_map/dot_general | solution.py:152
  193.5 27.2 %reduce-scatter.14.cloned.1.call-done = bf16[192,768]{1,0:T(8,128)(2,1)} async-done(((bf16[1536,768]{1,0:T(8,128)(2,1)}), bf16[192,768]{1,0:T(8,128)(2,1)}) %reduce-scatter.14.cloned.1.call-update) | async-done | bytes 294928
  (81 shorter events, 31.1 us)
Async XLA Ops:
  7.2 57.6 %copy-start = (bf16[1,768,1536]{2,1,0:T(8,128)(2,1)S(1)}, bf16[1,768,1536]{2,1,0:T(8,128)(2,1)}, u32[]{:S(2)}) copy-start(bf16[1,768,1536]{2,1,0:T(8,128)(2,1)} %param.19) | copy-start | bytes 7077892
  8.3 5.7 %collective-permute-start = (bf16[1,64,768]{2,1,0:T(8,128)(2,1)S(1)}, bf16[1,64,768]{2,1,0:T(8,128)(2,1)S(1)}, u32[]{:S(2)}, u32[]{:S(2)}) collective-permute-start(bf16[1,64,768]{2,1,0:T(8,128)(2,1)S(1)} %get-tuple-element.58), channel_id=1, source_target_pairs={{0,8},{8,16},{16,24},{24,32},{32,40},{40,48},{48,56},{56,64},{64,7... | collective-permute-start | bytes 294920 | tf_op jit(solution)/shard_map/ppermute | solution.py:14
  8.4 5.6 %collective-permute-start.1 = (bf16[1,64,768]{2,1,0:T(8,128)(2,1)S(1)}, bf16[1,64,768]{2,1,0:T(8,128)(2,1)S(1)}, u32[]{:S(2)}, u32[]{:S(2)}) collective-permute-start(bf16[1,64,768]{2,1,0:T(8,128)(2,1)S(1)} %get-tuple-element.59), channel_id=1, source_target_pairs={{8,0},{16,8},{24,16},{32,24},{40,32},{48,40},{56,48},{64,56},{72,6... | collective-permute-start | bytes 294920 | tf_op jit(solution)/shard_map/ppermute | solution.py:15
  13.9 4.1 %copy-start.9 = (f32[256]{0:T(256)}, f32[256]{0:T(256)S(1)}, u32[]{:S(2)}) copy-start(f32[256]{0:T(256)S(1)} %maximum_divide_fusion) | copy-start | bytes 3076
  15.2 2.9 %copy-start.7 = (f32[768]{0:T(1024)S(1)}, f32[768]{0:T(1024)}, u32[]{:S(2)}) copy-start(f32[768]{0:T(1024)} %param.17) | copy-start | bytes 9220
  15.2 3.0 %copy-start.4 = (bf16[1,256,768]{2,1,0:T(8,128)(2,1)S(1)}, bf16[1,256,768]{2,1,0:T(8,128)(2,1)}, u32[]{:S(2)}) copy-start(bf16[1,256,768]{2,1,0:T(8,128)(2,1)} %param.21) | copy-start | bytes 1179652
  42.1 19.2 %all-to-all-start.2 = ((bf16[32,16,768]{2,1,0:T(8,128)(2,1)}), bf16[32,16,768]{2,1,0:T(8,128)(2,1)}, u32[]{:S(2)}, u32[]{:S(2)}) async-start(bf16[32,16,768]{2,1,0:T(8,128)(2,1)} %bitcast.122), calls=%async_computation.2 | async-start | bytes 1572864 | tf_op jit(solution)/shard_map/all_to_all | solution.py:84
  48.6 139.4 %reduce-scatter.12.cloned.1.call-start = ((), (), s32[]{:S(2)}) async-start(), calls=%async_computation.8 | async-start | bytes 2654208
  61.3 3.5 %copy-start.6 = (bf16[32,16,768]{2,1,0:T(8,128)(2,1)S(1)}, bf16[32,16,768]{2,1,0:T(8,128)(2,1)}, u32[]{:S(2)}) copy-start(bf16[32,16,768]{2,1,0:T(8,128)(2,1)} %all_to_all.20) | copy-start | bytes 2359300
  61.3 3.5 %copy-start.13 = (f32[512,1536]{1,0:T(8,128)S(1)}, f32[512,1536]{1,0:T(8,128)}, u32[]{:S(2)}) copy-start(f32[512,1536]{1,0:T(8,128)} %fusion.14) | copy-start | bytes 9437188
  68.6 1.2 copy-start.14
  88.9 101.9 %reduce-scatter.10.cloned.1.call-start = ((), (), s32[]{:S(2)}) async-start(), calls=%async_computation.7 | async-start | bytes 2654208
  109.8 110.9 %reduce-scatter.14.cloned.1.call-start = ((), (), s32[]{:S(2)}) async-start(), calls=%async_computation.9 | async-start | bytes 2654208
  135.3 19.2 %all-to-all-start.1 = ((bf16[32,16,768]{2,1,0:T(8,128)(2,1)}), bf16[32,16,768]{2,1,0:T(8,128)(2,1)}, u32[]{:S(2)}, u32[]{:S(2)}) async-start(bf16[32,16,768]{2,1,0:T(8,128)(2,1)} %bitcast.129), calls=%async_computation.1 | async-start | bytes 1572864 | tf_op jit(solution)/shard_map/all_to_all | solution.py:106
  141.8 3.0 %copy-start.10 = (bf16[1,768,1536]{2,1,0:T(8,128)(2,1)S(1)}, bf16[1,768,1536]{2,1,0:T(8,128)(2,1)}, u32[]{:S(2)}) copy-start(bf16[1,768,1536]{2,1,0:T(8,128)(2,1)} %param.18) | copy-start | bytes 7077892
  141.8 3.0 %copy-start.15 = (bf16[512,1536]{1,0:T(8,128)(2,1)S(1)}, bf16[512,1536]{1,0:T(8,128)(2,1)}, u32[]{:S(2)}) copy-start(bf16[512,1536]{1,0:T(8,128)(2,1)} %get-tuple-element.50) | copy-start | bytes 4718596
  174.6 1.2 copy-start.2
  175.8 0.7 copy-start.8
  180.0 1.3 copy-start.1
  180.0 6.7 %slice-start = ((f32[384,768]{1,0:T(8,128)}), f32[256,768]{1,0:T(8,128)S(1)}, s32[]{:S(2)}) async-start(f32[384,768]{1,0:T(8,128)} %fusion.20), calls=%async_computation.10 | async-start | bytes 1572864 | tf_op jit(solution)/shard_map/slice | solution.py:157
  181.3 5.5 %copy-start.3 = (f32[256,1536]{1,0:T(8,128)S(1)}, f32[256,1536]{1,0:T(8,128)}, u32[]{:S(2)}) copy-start(f32[256,1536]{1,0:T(8,128)} %copy-done.2) | copy-start | bytes 4718596
  181.3 5.5 %copy-start.5 = (bf16[1,256,768]{2,1,0:T(8,128)(2,1)S(1)}, bf16[1,256,768]{2,1,0:T(8,128)(2,1)}, u32[]{:S(2)}) copy-start(bf16[1,256,768]{2,1,0:T(8,128)(2,1)} %param.13) | copy-start | bytes 1179652
  181.3 3.6 %collective-permute-start.3 = (bf16[1,64,768]{2,1,0:T(8,128)(2,1)S(1)}, bf16[1,64,768]{2,1,0:T(8,128)(2,1)S(1)}, u32[]{:S(2)}, u32[]{:S(2)}) collective-permute-start(bf16[1,64,768]{2,1,0:T(8,128)(2,1)S(1)} %bitcast.133), channel_id=1, source_target_pairs={{8,0},{16,8},{24,16},{32,24},{40,32},{48,40},{56,48},{64,56},{72,6... | collective-permute-start | bytes 294920 | tf_op jit(solution)/shard_map/ppermute | solution.py:15
  182.7 4.0 %collective-permute-start.2 = (bf16[1,64,768]{2,1,0:T(8,128)(2,1)S(1)}, bf16[1,64,768]{2,1,0:T(8,128)(2,1)S(1)}, u32[]{:S(2)}, u32[]{:S(2)}) collective-permute-start(bf16[1,64,768]{2,1,0:T(8,128)(2,1)S(1)} %bitcast.132), channel_id=1, source_target_pairs={{0,8},{8,16},{16,24},{24,32},{32,40},{40,48},{48,56},{56,64},{64,7... | collective-permute-start | bytes 294920 | tf_op jit(solution)/shard_map/ppermute | solution.py:14
  (2 other events, 1.3 us)
Sparse Core Ops, SparseCore 0:
  89.0 42.2 reduce-scatter.11
  133.8 42.2 reduce-scatter.9
  178.7 42.0 reduce-scatter.13
where the time goes:
time: 232 us; the launch traced here: 230 us
  local copies, waits for them, and re-layouts  64.8 us (28%)
  waiting for transfers between devices  46.2 us (20%)
  matrix products  42.5 us (18%)
  blocking collectives  40.7 us (18%)
  starting transfers between devices  16.5 us (7%)
  between operations  14 us (6%)
  other arithmetic  5.28 us (2%)
    unnamed x47, local copies, waits for them, and re-layouts  62.4 us
    unnamed x6, waiting for transfers between devices  27.2 us
    all_to_all x1, blocking collectives, on_device(): lax.all_to_all(send_rows, 'expert', split_axis=0, concat_axis=0, tiled=True)  22.3 us
    all_to_all x1, blocking collectives, on_device(): lax.all_to_all(d_rows.reshape(expert_count, capacity, width), 'expert', s...  18.5 us
    dot_general x3, matrix products, contract_rows(): lax.dot_general(left, right, (((0,), (0,)), ((), ())), preferred_element_...  11.9 us
    dot_general x3, matrix products, contract_last(): lax.dot_general(left, right, (((1,), (1,)), ((), ())), preferred_element_...  9.76 us
    all_to_all x1, waiting for transfers between devices, on_device(): lax.all_to_all(send_grads, 'expert', split_axis=0, concat_axis=0, tiled=T...  7.64 us
    all_to_all x1, waiting for transfers between devices, on_device(): lax.all_to_all(expert_out.reshape(expert_count, capacity, width), 'expert...  7.29 us
  transfers between devices with their start and end apart: 9, of which 5 were waited for; matrix products, arithmetic and copies ran while one was open for 32% of the time, Pallas kernels for 0%

commit v1 on v0

v1 whole, which is shorter than its diff:
```python
import jax
import jax.numpy as jnp
from jax import lax
from jax.experimental import pallas as pl
from jax.experimental.pallas import tpu as pltpu
from jax.sharding import PartitionSpec as P

MESH = pl.DeviceIdType.MESH
F32 = jnp.float32
BF16 = jnp.bfloat16

D = 768
FF = 1536
NODES = 256
RIM = 64
EXTENT = NODES + 2 * RIM
EDGES = 1024
EXPERTS = 32
CAP = 16
ROWS = EXPERTS * CAP
REPS = 8
SLICE = FF // REPS
HALF = D // 2


def partner_order():
    hops = (0, 1, 2, 1)
    offsets = [(a, b, c) for a in range(4) for b in range(4) for c in range(2)][1:]
    offsets.sort(key=lambda o: -(hops[o[0]] + hops[o[1]]))
    order = []
    for o in offsets:
        opposite = ((4 - o[0]) % 4, (4 - o[1]) % 4, o[2])
        for p in (o, opposite):
            if p not in order:
                order.append(p)
    return order


ORDER = partner_order()


def dot(a, b):
    return jnp.dot(a, b, preferred_element_type=F32)


def dot_last(a, b):
    return lax.dot_general(a, b, (((1,), (1,)), ((), ())), preferred_element_type=F32)


def chunk(i, size):
    return pl.ds(pl.multiple_of(i * size, size), size)


def kernel(
    nodes, sources, targets, codes, gain, w_gate, w_up, w_down, d_out,
    layer_out, d_nodes, grad_gate, grad_up, grad_down,
    wg, wu, wd, wgt, wut, wdt, partial, ring,
    send_g, send_r, recv_g, recv_r, back_e, back_d, ret_e, ret_d,
    hid_t, dgate_t, dup_t, bh_t, gate_s, up_s,
    normal, total, counts, counts_t, place, place_t, scale_s, inv_s,
    rim_in, rim_out, rim_back, dmean,
    w_sem, rim_send, rim_recv, a2a_send, a2a_recv, ring_send, ring_recv,
):
    me = lax.axis_index("expert")
    rep = lax.axis_index("rep")
    my, mx, mc = me // 8, lax.rem(me // 2, 4), lax.rem(me, 2)
    following, before = lax.rem(me + 1, EXPERTS), lax.rem(me + EXPERTS - 1, EXPERTS)
    rep_up, rep_down = lax.rem(rep + 1, REPS), lax.rem(rep + REPS - 1, REPS)

    def partner(offset):
        a, b, c = offset
        return lax.rem(my + a, 4) * 8 + lax.rem(mx + b, 4) * 2 + lax.rem(mc + c, 2)

    barrier = pltpu.get_barrier_semaphore()

    def greet(i, carry):
        pl.semaphore_signal(
            barrier, inc=1, device_id=(lax.rem(me + i, EXPERTS), rep), device_id_type=MESH
        )
        return carry

    lax.fori_loop(1, EXPERTS, greet, 0)
    for z in (rep_up, rep_down):
        pl.semaphore_signal(barrier, inc=1, device_id=(me, z), device_id_type=MESH)

    loads = [
        pltpu.make_async_copy(src, dst, w_sem.at[i])
        for i, (src, dst) in enumerate(((w_down, wd), (w_gate, wg), (w_up, wu)))
    ]
    for load in loads:
        load.start()

    code_row = codes[...].astype(F32)
    code_col = jnp.transpose(jnp.broadcast_to(code_row, (128, NODES)))[:, :1]
    first = lax.broadcasted_iota(jnp.int32, (NODES, NODES), 0)
    second = lax.broadcasted_iota(jnp.int32, (NODES, NODES), 1)
    same = code_col == code_row
    rank_row = jnp.sum(jnp.where(same & (first < second), 1.0, 0.0), axis=0, keepdims=True)
    rank_col = jnp.sum(jnp.where(same & (second < first), 1.0, 0.0), axis=1, keepdims=True)
    slot_row = (code_row * CAP + rank_row).astype(jnp.int32)
    slot_col = (code_col * CAP + rank_col).astype(jnp.int32)
    place_t[...] = jnp.where(
        lax.broadcasted_iota(jnp.int32, (ROWS, NODES), 0) == slot_row, 1.0, 0.0
    ).astype(BF16)
    place[...] = jnp.where(
        lax.broadcasted_iota(jnp.int32, (NODES, ROWS), 1) == slot_col, 1.0, 0.0
    ).astype(BF16)

    def bucket(rows, out):
        out[...] = dot(place_t[...], rows[...]).astype(BF16).reshape(EXPERTS, CAP, D)

    bucket(d_out, send_g)

    src = sources[...]
    src = jnp.where(src >= RIM, src - RIM, src + (EXTENT - RIM))
    source_hot = jnp.where(
        lax.broadcasted_iota(jnp.int32, (EXTENT, EDGES), 0) == src, 1.0, 0.0
    ).astype(BF16)
    target_hot = jnp.where(
        lax.broadcasted_iota(jnp.int32, (NODES, EDGES), 0) == targets[...], 1.0, 0.0
    ).astype(BF16)
    count = dot_last(target_hot, source_hot)
    counts[...] = count.astype(BF16)
    counts_t[...] = jnp.transpose(count).astype(BF16)
    inv_s[...] = 1.0 / jnp.maximum(jnp.sum(count, axis=1, keepdims=True), 1.0)

    pl.semaphore_wait(barrier, EXPERTS + 1)

    def rim_copies(low, high, landing, base):
        return [
            pltpu.make_async_remote_copy(
                low, landing.at[pl.ds(0, RIM)], rim_send.at[base], rim_recv.at[base],
                device_id=(before, rep), device_id_type=MESH,
            ),
            pltpu.make_async_remote_copy(
                high, landing.at[pl.ds(RIM, RIM)], rim_send.at[base + 1], rim_recv.at[base + 1],
                device_id=(following, rep), device_id_type=MESH,
            ),
        ]

    rim_first = rim_copies(nodes.at[pl.ds(0, RIM)], nodes.at[pl.ds(NODES - RIM, RIM)], rim_in, 0)
    for copy in rim_first:
        copy.start()

    def exchange(source, landing, slot):
        for offset in ORDER:
            t = partner(offset)
            pltpu.make_async_remote_copy(
                source.at[t], landing.at[me], a2a_send.at[slot], a2a_recv.at[slot],
                device_id=(t, rep), device_id_type=MESH,
            ).start()
        landing[me] = source[me]

    def exchange_wait(landing, slot):
        part = landing.at[pl.ds(0, EXPERTS - 1)]
        pltpu.make_async_copy(part, part, a2a_recv.at[slot]).wait()

    def exchange_sent(source, slot):
        part = source.at[pl.ds(0, EXPERTS - 1)]
        pltpu.make_async_copy(part, part, a2a_send.at[slot]).wait()

    exchange(send_g, recv_g, 0)

    total[...] = dot(counts[:, pl.ds(0, NODES)], nodes[...])
    for copy in rim_first:
        copy.wait_recv()
    total[...] += dot(counts[:, pl.ds(NODES, 2 * RIM)], rim_in[...])

    def normalize(i, carry):
        at = chunk(i, 32)
        mixed = nodes[at, :].astype(F32) + total[at, :] * inv_s[at, :]
        scaling = lax.rsqrt(jnp.mean(mixed * mixed, axis=1, keepdims=True) + 1e-05)
        scale_s[at, :] = scaling
        norm = mixed * scaling
        normal[at, :] = norm
        dmean[at, :] = (norm * gain[...]).astype(BF16)
        return carry

    lax.fori_loop(0, NODES // 32, normalize, 0)
    bucket(dmean, send_r)
    exchange(send_r, recv_r, 1)

    def turn(source, out):
        def body(i, carry):
            out[chunk(i, 128), :] = jnp.transpose(source[:, chunk(i, 128)])
            return carry

        lax.fori_loop(0, FF // 128, body, 0)

    loads[0].wait()
    turn(wd, wdt)
    loads[1].wait()
    turn(wg, wgt)
    loads[2].wait()
    turn(wu, wut)

    exchange_wait(recv_g, 0)

    def flat(ref):
        return ref[...].reshape(ROWS, D)

    def back(i, carry):
        at = chunk(i, SLICE)
        bh_t[at, :] = dot_last(wdt[at, :], flat(recv_g))
        return carry

    lax.fori_loop(0, REPS, back, 0)
    exchange_wait(recv_r, 1)

    def expert_slice(c):
        base = pl.multiple_of(c * SLICE, SLICE)
        at = pl.ds(base, SLICE)
        gate_s[...] = dot_last(wgt[at, :], flat(recv_r))
        up_s[...] = dot_last(wut[at, :], flat(recv_r))

        def act(i, carry):
            rows = chunk(i, 16)
            here = pl.ds(pl.multiple_of(base + i * 16, 16), 16)
            g, u, b = gate_s[rows, :], up_s[rows, :], bh_t[here, :]
            s = jax.nn.sigmoid(g)
            silu = g * s
            hid_t[here, :] = (silu * u).astype(BF16)
            dgate_t[here, :] = (b * u * s * (1.0 + g * (1.0 - s))).astype(BF16)
            dup_t[here, :] = (b * silu).astype(BF16)
            return carry

        lax.fori_loop(0, SLICE // 16, act, 0)
        for j, (left, right) in enumerate(
            ((hid_t, recv_g), (dgate_t, recv_r), (dup_t, recv_r))
        ):
            g = dot(left[at, :], flat(right)).astype(BF16)
            partial[c, j, 0] = g[:, :HALF]
            partial[c, j, 1] = g[:, HALF:]

    def mod(i):
        return lax.rem(i + 2 * REPS, REPS)

    def piece(d, k):
        return mod(rep - 1 - k) if d == 0 else mod(rep + 1 + k)

    def hop(d, k, j):
        source = partial.at[piece(d, 0), j, d] if k == 0 else ring.at[k - 1, j, d]
        return pltpu.make_async_remote_copy(
            source, ring.at[k, j, d], ring_send.at[k, j, d], ring_recv.at[k, j, d],
            device_id=(me, rep_up if d == 0 else rep_down), device_id_type=MESH,
        )

    def serve(k, j):
        for d in range(2):
            hop(d, k - 1, j).wait_recv()
            c = piece(d, k)

            def add(i, carry):
                at = chunk(i, 32)
                ring[k - 1, j, d, at, :] = (
                    ring[k - 1, j, d, at, :].astype(F32) + partial[c, j, d, at, :].astype(F32)
                ).astype(BF16)
                return carry

            lax.fori_loop(0, SLICE // 32, add, 0)
            hop(d, k, j).start()

    def pair(i):
        other = mod(rep + 1 + i) if i < 3 else rep

        def body(s, carry):
            expert_slice(jnp.where(s == 0, mod(rep - 1 - i), other))
            return carry

        lax.fori_loop(0, 2, body, 0)

    pair(0)
    for j in range(3):
        for d in range(2):
            hop(d, 0, j).start()
    pair(1)
    serve(1, 0)
    pair(2)
    serve(1, 1)
    pair(3)
    serve(1, 2)

    def project(terms, out):
        def body(b, carry):
            at = chunk(b, 256)
            y = dot(terms[0][0][at, :], terms[0][1][...])
            for w, x in terms[1:]:
                y = y + dot(w[at, :], x[...])
            out[:, :, at] = jnp.transpose(y).astype(BF16).reshape(EXPERTS, CAP, 256)
            return carry

        lax.fori_loop(0, D // 256, body, 0)

    project(((wd, hid_t),), back_e)
    exchange(back_e, ret_e, 2)
    serve(2, 0)
    project(((wg, dgate_t), (wu, dup_t)), back_d)
    exchange(back_d, ret_d, 3)
    serve(2, 1)
    serve(2, 2)
    for j in range(3):
        serve(3, j)
    for j in range(3):
        serve(4, j)

    exchange_wait(ret_e, 2)
    total[...] = dot(place[...], flat(ret_e))

    def forward_out(i, carry):
        at = chunk(i, 32)
        layer_out[at, :] = (nodes[at, :].astype(F32) + total[at, :]).astype(BF16)
        return carry

    lax.fori_loop(0, NODES // 32, forward_out, 0)
    exchange_wait(ret_d, 3)
    total[...] = dot(place[...], flat(ret_d))
    serve(5, 0)

    def norm_back(i, carry):
        at = chunk(i, 32)
        d_norm = total[at, :] * gain[...]
        norm = normal[at, :]
        d_mixed = scale_s[at, :] * (d_norm - norm * jnp.mean(d_norm * norm, axis=1, keepdims=True))
        dmean[at, :] = (d_mixed * inv_s[at, :]).astype(BF16)
        total[at, :] = d_out[at, :].astype(F32) + d_mixed
        return carry

    lax.fori_loop(0, NODES // 32, norm_back, 0)
    rim_out[...] = dot(counts_t[pl.ds(NODES, 2 * RIM), :], dmean[...]).astype(BF16)
    rim_last = rim_copies(rim_out.at[pl.ds(RIM, RIM)], rim_out.at[pl.ds(0, RIM)], rim_back, 2)
    for copy in rim_last:
        copy.start()
    serve(5, 1)
    total[...] += dot(counts_t[pl.ds(0, NODES), :], dmean[...])
    serve(5, 2)
    for copy in rim_last:
        copy.wait_recv()
    total[pl.ds(0, RIM), :] += rim_back[pl.ds(RIM, RIM), :].astype(F32)
    total[pl.ds(NODES - RIM, RIM), :] += rim_back[pl.ds(0, RIM), :].astype(F32)
    serve(6, 0)

    def node_out(i, carry):
        at = chunk(i, 32)
        d_nodes[at, :] = total[at, :].astype(BF16)
        return carry

    lax.fori_loop(0, NODES // 32, node_out, 0)
    serve(6, 1)
    serve(6, 2)
    for j, out in enumerate((grad_down, grad_gate, grad_up)):
        for d in range(2):
            hop(d, 6, j).wait_recv()
            y = ring[6, j, d].astype(F32) + partial[rep, j, d].astype(F32)
            out[pl.ds(d * HALF, HALF), :] = jnp.transpose(y)

    for copy in rim_first + rim_last:
        copy.wait_send()
    for slot, source in enumerate((send_g, send_r, back_e, back_d)):
        exchange_sent(source, slot)
    for k in range(REPS - 1):
        for j in range(3):
            for d in range(2):
                hop(d, k, j).wait_send()


def on_device(node_feats, edge_src, edge_dst, node_codes, norm_gain, w_gate, w_up, w_down_t, d_out):
    vmem, hbm = pl.BlockSpec(memory_space=pltpu.VMEM), pl.BlockSpec(memory_space=pl.ANY)
    weight = pltpu.VMEM((D, FF), BF16)
    weight_t = pltpu.VMEM((FF, D), BF16)
    buckets = pltpu.VMEM((EXPERTS, CAP, D), BF16)
    act_t = pltpu.VMEM((FF, ROWS), BF16)
    rims = pltpu.VMEM((2 * RIM, D), BF16)
    sem = pltpu.SemaphoreType.DMA
    out = pl.pallas_call(
        kernel,
        out_shape=[jax.ShapeDtypeStruct((NODES, D), BF16)] * 2
        + [jax.ShapeDtypeStruct((D, SLICE), F32)] * 3,
        in_specs=[vmem] * 5 + [hbm] * 3 + [vmem],
        out_specs=[vmem] * 5,
        scratch_shapes=[weight] * 3
        + [weight_t] * 3
        + [
            pltpu.VMEM((REPS, 3, 2, SLICE, HALF), BF16),
            pltpu.VMEM((REPS - 1, 3, 2, SLICE, HALF), BF16),
        ]
        + [buckets] * 8
        + [act_t] * 3
        + [
            pltpu.VMEM((FF, ROWS), F32),
            pltpu.VMEM((SLICE, ROWS), F32),
            pltpu.VMEM((SLICE, ROWS), F32),
            pltpu.VMEM((NODES, D), F32),
            pltpu.VMEM((NODES, D), F32),
            pltpu.VMEM((NODES, EXTENT), BF16),
            pltpu.VMEM((EXTENT, NODES), BF16),
            pltpu.VMEM((NODES, ROWS), BF16),
            pltpu.VMEM((ROWS, NODES), BF16),
            pltpu.VMEM((NODES, 1), F32),
            pltpu.VMEM((NODES, 1), F32),
        ]
        + [rims] * 3
        + [
            pltpu.VMEM((NODES, D), BF16),
            sem((3,)),
            sem((4,)),
            sem((4,)),
            sem((4,)),
            sem((4,)),
            sem((REPS - 1, 3, 2)),
            sem((REPS - 1, 3, 2)),
        ],
        compiler_params=pltpu.CompilerParams(
            collective_id=0, has_side_effects=True, vmem_limit_bytes=60 * 2**20
        ),
        name="graph_moe",
    )(
        node_feats[0], edge_src, edge_dst, node_codes.reshape(1, NODES), norm_gain.reshape(1, D),
        w_gate[0], w_up[0], w_down_t[0], d_out[0],
    )
    return tuple(x[None] for x in out)


def solution(mesh):
    rows = P("rep", "expert", None)
    edges = P("rep", "expert")
    weights = P("expert", None, None)
    grads = P("expert", None, "rep")
    return jax.shard_map(
        on_device,
        mesh=mesh,
        in_specs=(rows, edges, edges, rows, P(), weights, weights, weights, rows),
        out_specs=(rows, rows, grads, grads, grads),
        check_vma=False,
    )
```

time: 232 us -> 116 us (0.50)
  the two profiles are of different devices: /device:TPU:4 before, /device:TPU:1 now
where the time goes in v1:
time: 116 us
  Pallas kernels  107 us (92%)
  local copies, waits for them, and re-layouts  8.35 us (7%)
    pallas_call x1, Pallas kernels, on_device(): pl.pallas_call(kernel, out_shape=[jax.ShapeDtypeStruct((NODES, D), BF16)]...  107 us
    unnamed x11, local copies, waits for them, and re-layouts  7.08 us

profile of v1, /device:TPU:1, one launch (start us, length us, event | category | flops | bytes accessed | tf_op | source)
XLA Modules:
  0.0 115.7 jit_solution(8134149513120627534)
XLA Ops:
  0.6 1.3 %reshape.17.gain = f32[1,768]{1,0:T(1,128)} reshape(f32[768]{0:T(1024)} %param.13) | data formatting | bytes 6144 | tf_op jit(solution)/shard_map/reshape | solution.py:417
  1.9 106.7 %graph_moe.1 = (bf16[256,768]{1,0:T(8,128)(2,1)}, bf16[256,768]{1,0:T(8,128)(2,1)}, f32[768,192]{1,0:T(8,128)}, f32[768,192]{1,0:T(8,128)}, f32[768,192]{1,0:T(8,128)}) custom-call(bf16[256,768]{1,0:T(8,128)(2,1)} %bitcast.17, s32[1,1024]{1,0:T(1,128)} %sources.1, s32[1,1024]{1,0:T(1,128)} %targets.1, s32[1,256]{1,0:T(1,128)} %bitcast.21, ...), custom_call_target="tpu_custom_call" | custom-call | tf_op jit(solution)/shard_map/graph_moe/pallas_call | solution.py:374
  108.6 0.0 copy-start
  108.6 0.0 copy-start.2
  108.6 0.0 copy-start.1
  108.6 2.3 %copy.14 = f32[1,768,192]{1,2,0:T(8,128)} copy(f32[1,768,192]{2,1,0:T(8,128)} %bitcast.16) | data formatting | bytes 1179648
  110.9 2.2 %copy.15 = f32[1,768,192]{1,2,0:T(8,128)} copy(f32[1,768,192]{2,1,0:T(8,128)} %bitcast.15) | data formatting | bytes 1179648
  113.1 0.0 copy-done
  113.1 1.1 copy.16
  114.2 0.0 copy-done.2
  114.2 0.7 copy.19
  114.9 0.0 copy-done.1
  114.9 0.7 copy.20
Async XLA Ops:
  108.6 4.5 %copy-start = (f32[768,192]{1,0:T(8,128)S(1)}, f32[768,192]{1,0:T(8,128)}, u32[]{:S(2)}) copy-start(f32[768,192]{1,0:T(8,128)} %get-tuple-element.14) | copy-start | bytes 1769476
  108.6 5.6 %copy-start.2 = (bf16[256,768]{1,0:T(8,128)(2,1)S(1)}, bf16[256,768]{1,0:T(8,128)(2,1)}, u32[]{:S(2)}) copy-start(bf16[256,768]{1,0:T(8,128)(2,1)} %get-tuple-element.10) | copy-start | bytes 1179652
  108.6 6.3 %copy-start.1 = (bf16[256,768]{1,0:T(8,128)(2,1)S(1)}, bf16[256,768]{1,0:T(8,128)(2,1)}, u32[]{:S(2)}) copy-start(bf16[256,768]{1,0:T(8,128)(2,1)} %get-tuple-element.11) | copy-start | bytes 1179652

commit v2 on v1

v2 whole, which is shorter than its diff:
```python
import jax
import jax.numpy as jnp
from jax import lax
from jax.experimental import pallas as pl
from jax.experimental.pallas import tpu as pltpu
from jax.sharding import PartitionSpec as P

MESH = pl.DeviceIdType.MESH
F32 = jnp.float32
BF16 = jnp.bfloat16

D = 768
FF = 1536
NODES = 256
RIM = 64
EXTENT = NODES + 2 * RIM
EDGES = 1024
EXPERTS = 32
CAP = 16
ROWS = EXPERTS * CAP
REPS = 8
SLICE = FF // REPS
PART = SLICE // 2


def partner_order():
    hops = (0, 1, 2, 1)
    offsets = [(a, b) for a in range(4) for b in range(4)][1:]
    offsets.sort(key=lambda o: -(hops[o[0]] + hops[o[1]]))
    order = []
    for a, b in offsets:
        for p in ((a, b), ((4 - a) % 4, (4 - b) % 4)):
            if p not in order:
                order.append(p)
    return order


ORDER = partner_order()
CHIPS = len(ORDER)


def dot(a, b):
    return jnp.dot(a, b, preferred_element_type=F32)


def dot_last(a, b):
    return lax.dot_general(a, b, (((1,), (1,)), ((), ())), preferred_element_type=F32)


def chunk(i, size):
    return pl.ds(pl.multiple_of(i * size, size), size)


def kernel(
    nodes_hbm, sources_hbm, targets_hbm, codes_hbm, gain_hbm, w_gate, w_up, w_down, d_out_hbm,
    layer_out, d_nodes, grad_gate, grad_up, grad_down,
    nodes, sources, targets, codes, gain, d_out,
    wg, wu, wd, wgt, wut, wdt, partial, ring,
    send_g, send_r, recv_g, recv_r, back_e, back_d, ret_e, ret_d,
    hid_t, dgate_t, dup_t, bh_s, gate_s, up_s,
    normal, total, counts, counts_t, place, place_t, scale_s, inv_s,
    rim_in, rim_out, rim_back, dmean,
    load_sem, rim_send, rim_recv, a2a_send, a2a_recv, ring_send, ring_recv,
):
    me = lax.axis_index("expert")
    rep = lax.axis_index("rep")
    my, mx, mc = me // 8, lax.rem(me // 2, 4), lax.rem(me, 2)
    following, before = lax.rem(me + 1, EXPERTS), lax.rem(me + EXPERTS - 1, EXPERTS)
    rep_up, rep_down = lax.rem(rep + 1, REPS), lax.rem(rep + REPS - 1, REPS)

    barrier = pltpu.get_barrier_semaphore()

    def greet(i, carry):
        pl.semaphore_signal(
            barrier, inc=1, device_id=(lax.rem(me + i, EXPERTS), rep), device_id_type=MESH
        )
        return carry

    lax.fori_loop(1, EXPERTS, greet, 0)
    for z in (rep_up, rep_down):
        pl.semaphore_signal(barrier, inc=1, device_id=(me, z), device_id_type=MESH)

    pairs = (
        (codes_hbm, codes), (d_out_hbm, d_out), (sources_hbm, sources), (targets_hbm, targets),
        (nodes_hbm, nodes), (gain_hbm, gain), (w_down, wd), (w_gate, wg), (w_up, wu),
    )
    loads = [pltpu.make_async_copy(x, y, load_sem.at[i]) for i, (x, y) in enumerate(pairs)]
    for load in loads:
        load.start()

    loads[0].wait()
    code_row = codes[...].astype(F32)
    code_col = jnp.transpose(jnp.broadcast_to(code_row, (128, NODES)))[:, :1]
    first = lax.broadcasted_iota(jnp.int32, (NODES, NODES), 0)
    second = lax.broadcasted_iota(jnp.int32, (NODES, NODES), 1)
    same = code_col == code_row
    rank_row = jnp.sum(jnp.where(same & (first < second), 1.0, 0.0), axis=0, keepdims=True)
    slot_row = (code_row * CAP + rank_row).astype(jnp.int32)
    place_t[...] = jnp.where(
        lax.broadcasted_iota(jnp.int32, (ROWS, NODES), 0) == slot_row, 1.0, 0.0
    ).astype(BF16)

    def bucket(rows, out):
        out[...] = dot(place_t[...], rows[...]).astype(BF16).reshape(EXPERTS, CAP, D)

    loads[1].wait()
    bucket(d_out, send_g)
    loads[4].wait()
    pl.semaphore_wait(barrier, EXPERTS + 1)

    def rim_copies(low, high, landing, base):
        return [
            pltpu.make_async_remote_copy(
                low, landing.at[pl.ds(0, RIM)], rim_send.at[base], rim_recv.at[base],
                device_id=(before, rep), device_id_type=MESH,
            ),
            pltpu.make_async_remote_copy(
                high, landing.at[pl.ds(RIM, RIM)], rim_send.at[base + 1], rim_recv.at[base + 1],
                device_id=(following, rep), device_id_type=MESH,
            ),
        ]

    rim_first = rim_copies(nodes.at[pl.ds(0, RIM)], nodes.at[pl.ds(NODES - RIM, RIM)], rim_in, 0)
    for copy in rim_first:
        copy.start()

    def exchange(source, landing, slot, core):
        def send(t, sem):
            pltpu.make_async_remote_copy(
                source.at[t], landing.at[me], sem, a2a_recv.at[slot],
                device_id=(t, rep), device_id_type=MESH,
            ).start()

        for a, b in ORDER:
            chip = lax.rem(my + a, 4) * 4 + lax.rem(mx + b, 4)
            send(chip * 2 + core, a2a_send.at[slot, core])

        @pl.when(mc != core)
        def _():
            send(my * 8 + mx * 2 + core, a2a_send.at[slot, 2])

    def exchange_wait(landing, slot):
        part = landing.at[pl.ds(0, EXPERTS - 1)]
        pltpu.make_async_copy(part, part, a2a_recv.at[slot]).wait()

    def exchange_sent(source, slot, core):
        part = source.at[pl.ds(0, CHIPS)]
        pltpu.make_async_copy(part, part, a2a_send.at[slot, core]).wait()

    exchange(send_g, recv_g, 0, 0)
    recv_g[me] = send_g[me]

    loads[2].wait()
    loads[3].wait()
    src = sources[...]
    src = jnp.where(src >= RIM, src - RIM, src + (EXTENT - RIM))
    source_hot = jnp.where(
        lax.broadcasted_iota(jnp.int32, (EXTENT, EDGES), 0) == src, 1.0, 0.0
    ).astype(BF16)
    target_hot = jnp.where(
        lax.broadcasted_iota(jnp.int32, (NODES, EDGES), 0) == targets[...], 1.0, 0.0
    ).astype(BF16)
    count = dot_last(target_hot, source_hot)
    counts[...] = count.astype(BF16)
    inv_s[...] = 1.0 / jnp.maximum(jnp.sum(count, axis=1, keepdims=True), 1.0)
    total[...] = dot(counts[:, pl.ds(0, NODES)], nodes[...])
    loads[5].wait()
    for copy in rim_first:
        copy.wait_recv()
    total[...] += dot(counts[:, pl.ds(NODES, 2 * RIM)], rim_in[...])
    gain_row = gain[...].reshape(1, D)

    def normalize(i, carry):
        at = chunk(i, 32)
        mixed = nodes[at, :].astype(F32) + total[at, :] * inv_s[at, :]
        scaling = lax.rsqrt(jnp.mean(mixed * mixed, axis=1, keepdims=True) + 1e-05)
        scale_s[at, :] = scaling
        norm = mixed * scaling
        normal[at, :] = norm
        dmean[at, :] = (norm * gain_row).astype(BF16)
        return carry

    lax.fori_loop(0, NODES // 32, normalize, 0)
    bucket(dmean, send_r)
    exchange(send_r, recv_r, 1, 0)
    recv_r[me] = send_r[me]

    def turn(source, out):
        def body(i, carry):
            out[chunk(i, 128), :] = jnp.transpose(source[:, chunk(i, 128)])
            return carry

        lax.fori_loop(0, FF // 128, body, 0)

    loads[6].wait()
    turn(wd, wdt)
    for slot, source in enumerate((send_g, send_r)):
        exchange_sent(source, slot, 0)
    exchange(send_g, recv_g, 0, 1)
    exchange(send_r, recv_r, 1, 1)
    loads[7].wait()
    turn(wg, wgt)
    loads[8].wait()
    turn(wu, wut)

    def flat(ref):
        return ref[...].reshape(ROWS, D)

    def mod(i):
        return lax.rem(i + 2 * REPS, REPS)

    def parts(i):
        low = mod(rep - 1 - i) * SLICE
        high = mod(rep + 1 + i) * SLICE + PART
        return [pl.ds(pl.multiple_of(x, PART), PART) for x in (low, high)]

    def item_rows(i, ref):
        low, high = parts(i)
        return jnp.concatenate([ref[low, :], ref[high, :]], axis=0)

    def hop(d, k, j):
        source = partial.at[0, j, d] if k == 0 else ring.at[k - 1, j, d]
        return pltpu.make_async_remote_copy(
            source, ring.at[k, j, d], ring_send.at[k, j, d], ring_recv.at[k, j, d],
            device_id=(me, rep_up if d == 0 else rep_down), device_id_type=MESH,
        )

    def item_back(i):
        bh_s[...] = dot_last(item_rows(i, wdt), flat(recv_g))

    def item(i, back=True):
        gate_s[...] = dot_last(item_rows(i, wgt), flat(recv_r))
        up_s[...] = dot_last(item_rows(i, wut), flat(recv_r))
        if back:
            item_back(i)
        for d, units in enumerate(parts(i)):

            def act(n, carry):
                rows = pl.ds(pl.multiple_of(d * PART + n * 16, 16), 16)
                here = pl.ds(pl.multiple_of(units.start + n * 16, 16), 16)
                g, u, b = gate_s[rows, :], up_s[rows, :], bh_s[rows, :]
                s = jax.nn.sigmoid(g)
                silu = g * s
                hid_t[here, :] = (silu * u).astype(BF16)
                dgate_t[here, :] = (b * u * s * (1.0 + g * (1.0 - s))).astype(BF16)
                dup_t[here, :] = (b * silu).astype(BF16)
                return carry

            lax.fori_loop(0, PART // 16, act, 0)
        for j, (left, right) in enumerate(((hid_t, recv_g), (dgate_t, recv_r), (dup_t, recv_r))):
            g = dot(item_rows(i, left), flat(right)).astype(BF16)
            for d in range(2):
                partial[i, j, d] = g[d * PART : (d + 1) * PART, :]
            if i == 0:
                for d in range(2):
                    hop(d, 0, j).start()

    def serve(k, j):
        for d in range(2):
            hop(d, k - 1, j).wait_recv()

            def add(i, carry):
                at = chunk(i, 16)
                ring[k - 1, j, d, at, :] = (
                    ring[k - 1, j, d, at, :].astype(F32) + partial[k, j, d, at, :].astype(F32)
                ).astype(BF16)
                return carry

            lax.fori_loop(0, PART // 16, add, 0)
            hop(d, k, j).start()

    exchange_wait(recv_g, 0)
    item_back(0)
    exchange_wait(recv_r, 1)
    item(0, back=False)
    item(1)
    item(2)
    serve(1, 0)
    serve(1, 1)
    item(3)
    serve(1, 2)
    item(4)
    serve(2, 0)
    item(5)
    serve(2, 1)
    item(6)
    serve(2, 2)
    item(7)
    serve(3, 0)

    def project(terms, out):
        def body(b, carry):
            at = chunk(b, 256)
            y = dot(terms[0][0][at, :], terms[0][1][...])
            for w, x in terms[1:]:
                y = y + dot(w[at, :], x[...])
            out[:, :, at] = jnp.transpose(y).astype(BF16).reshape(EXPERTS, CAP, 256)
            return carry

        lax.fori_loop(0, D // 256, body, 0)

    project(((wd, hid_t),), back_e)
    for core in range(2):
        exchange(back_e, ret_e, 2, core)
    ret_e[me] = back_e[me]
    serve(3, 1)
    project(((wg, dgate_t), (wu, dup_t)), back_d)
    for core in range(2):
        exchange(back_d, ret_d, 3, core)
    ret_d[me] = back_d[me]
    serve(3, 2)
    serve(4, 0)
    rank_col = jnp.sum(jnp.where(same & (second < first), 1.0, 0.0), axis=1, keepdims=True)
    slot_col = (code_col * CAP + rank_col).astype(jnp.int32)
    place[...] = jnp.where(
        lax.broadcasted_iota(jnp.int32, (NODES, ROWS), 1) == slot_col, 1.0, 0.0
    ).astype(BF16)
    counts_t[...] = jnp.transpose(counts[...].astype(F32)).astype(BF16)
    serve(4, 1)
    serve(4, 2)
    for j in range(3):
        serve(5, j)

    exchange_wait(ret_e, 2)
    total[...] = dot(place[...], flat(ret_e))

    def forward_out(i, carry):
        at = chunk(i, 32)
        layer_out[at, :] = (nodes[at, :].astype(F32) + total[at, :]).astype(BF16)
        return carry

    lax.fori_loop(0, NODES // 32, forward_out, 0)
    exchange_wait(ret_d, 3)
    total[...] = dot(place[...], flat(ret_d))

    def norm_back(i, carry):
        at = chunk(i, 32)
        d_norm = total[at, :] * gain_row
        norm = normal[at, :]
        d_mixed = scale_s[at, :] * (d_norm - norm * jnp.mean(d_norm * norm, axis=1, keepdims=True))
        dmean[at, :] = (d_mixed * inv_s[at, :]).astype(BF16)
        total[at, :] = d_out[at, :].astype(F32) + d_mixed
        return carry

    lax.fori_loop(0, NODES // 32, norm_back, 0)
    rim_out[...] = dot(counts_t[pl.ds(NODES, 2 * RIM), :], dmean[...]).astype(BF16)
    rim_last = rim_copies(rim_out.at[pl.ds(RIM, RIM)], rim_out.at[pl.ds(0, RIM)], rim_back, 2)
    for copy in rim_last:
        copy.start()
    serve(6, 0)
    total[...] += dot(counts_t[pl.ds(0, NODES), :], dmean[...])
    serve(6, 1)
    serve(6, 2)
    for copy in rim_last:
        copy.wait_recv()
    total[pl.ds(0, RIM), :] += rim_back[pl.ds(RIM, RIM), :].astype(F32)
    total[pl.ds(NODES - RIM, RIM), :] += rim_back[pl.ds(0, RIM), :].astype(F32)

    def node_out(i, carry):
        at = chunk(i, 32)
        d_nodes[at, :] = total[at, :].astype(BF16)
        return carry

    lax.fori_loop(0, NODES // 32, node_out, 0)
    for copy in rim_first + rim_last:
        copy.wait_send()
    for slot, source in enumerate((send_g, send_r, back_e, back_d)):
        for core in range(2):
            if slot > 1 or core == 1:
                exchange_sent(source, slot, core)
        part = source.at[0]
        pltpu.make_async_copy(part, part, a2a_send.at[slot, 2]).wait()
    for k in range(REPS - 2):
        for j in range(3):
            for d in range(2):
                hop(d, k, j).wait_send()

    for j, out in enumerate((grad_down, grad_gate, grad_up)):
        for d in range(2):
            hop(d, 6, j).wait_recv()

            def last(i, carry):
                at = chunk(i, 16)
                out[pl.ds(pl.multiple_of(d * PART + i * 16, 16), 16), :] = (
                    ring[6, j, d, at, :].astype(F32) + partial[7, j, d, at, :].astype(F32)
                )
                return carry

            lax.fori_loop(0, PART // 16, last, 0)
    for j in range(3):
        for d in range(2):
            hop(d, 6, j).wait_send()


def on_device(node_feats, edge_src, edge_dst, node_codes, norm_gain, w_gate, w_up, w_down_t, d_out):
    hbm = pl.BlockSpec(memory_space=pl.ANY)
    vmem = pltpu.VMEM
    sem = pltpu.SemaphoreType.DMA
    weight = vmem((D, FF), BF16)
    weight_t = vmem((FF, D), BF16)
    buckets = vmem((EXPERTS, CAP, D), BF16)
    act_t = vmem((FF, ROWS), BF16)
    rows = vmem((NODES, D), BF16)
    wide = vmem((NODES, D), F32)
    item = vmem((SLICE, ROWS), F32)
    rims = vmem((2 * RIM, D), BF16)
    outs = [jax.ShapeDtypeStruct((NODES, D), BF16)] * 2 + [
        jax.ShapeDtypeStruct((SLICE, D), F32)
    ] * 3
    out = pl.pallas_call(
        kernel,
        out_shape=[vmem(x.shape, x.dtype) for x in outs],
        in_specs=[hbm] * 9,
        out_specs=[pl.BlockSpec(memory_space=vmem)] * 5,
        scratch_shapes=[
            rows,
            vmem((1, EDGES), jnp.int32),
            vmem((1, EDGES), jnp.int32),
            vmem((1, NODES), jnp.int32),
            vmem((D,), F32),
            rows,
        ]
        + [weight] * 3
        + [weight_t] * 3
        + [vmem((REPS, 3, 2, PART, D), BF16), vmem((REPS - 1, 3, 2, PART, D), BF16)]
        + [buckets] * 8
        + [act_t] * 3
        + [item] * 3
        + [
            wide,
            wide,
            vmem((NODES, EXTENT), BF16),
            vmem((EXTENT, NODES), BF16),
            vmem((NODES, ROWS), BF16),
            vmem((ROWS, NODES), BF16),
            vmem((NODES, 1), F32),
            vmem((NODES, 1), F32),
        ]
        + [rims] * 3
        + [
            rows,
            sem((9,)),
            sem((4,)),
            sem((4,)),
            sem((4, 3)),
            sem((4,)),
            sem((REPS - 1, 3, 2)),
            sem((REPS - 1, 3, 2)),
        ],
        compiler_params=pltpu.CompilerParams(
            collective_id=0, has_side_effects=True, vmem_limit_bytes=58 * 2**20
        ),
        name="graph_moe",
    )(
        node_feats[0], edge_src, edge_dst, node_codes.reshape(1, NODES), norm_gain,
        w_gate[0], w_up[0], w_down_t[0], d_out[0],
    )
    layer_out, d_nodes, *grads = out
    return (layer_out[None], d_nodes[None], *(g.T[None] for g in grads))


def solution(mesh):
    rows = P("rep", "expert", None)
    edges = P("rep", "expert")
    weights = P("expert", None, None)
    grads = P("expert", None, "rep")
    return jax.shard_map(
        on_device,
        mesh=mesh,
        in_specs=(rows, edges, edges, rows, P(), weights, weights, weights, rows),
        out_specs=(rows, rows, grads, grads, grads),
        check_vma=False,
    )
```

time: 116 us -> 104 us (0.90)
  Pallas kernels: 107 us -> 99.4 us
  local copies, waits for them, and re-layouts: 8.35 us -> 3.94 us
    pallas_call x1, Pallas kernels: 107 us -> 99.4 us  [on_device(): pl.pallas_call(kernel, out_shape=[vmem(x.shape, x.dtype) for x in outs],...]
    unnamed x11 -> x5, local copies, waits for them, and re-layouts: 7.08 us -> 3.94 us
    reshape x1 -> x0, local copies, waits for them, and re-layouts: 1.27 us -> none  [on_device(): norm_gain.reshape(1, D)]
where the time goes in v2:
time: 104 us
  Pallas kernels  99.4 us (96%)
  local copies, waits for them, and re-layouts  3.94 us (4%)
    pallas_call x1, Pallas kernels, on_device(): pl.pallas_call(kernel, out_shape=[vmem(x.shape, x.dtype) for x in outs],...  99.4 us
    unnamed x5, local copies, waits for them, and re-layouts  3.94 us

profile of v2, /device:TPU:1, one launch (start us, length us, event | category | flops | bytes accessed | tf_op | source)
XLA Modules:
  0.0 104.0 jit_solution(11045530028118217313)
XLA Ops:
  0.6 99.4 %graph_moe.1 = (bf16[256,768]{1,0:T(8,128)(2,1)S(1)}, bf16[256,768]{1,0:T(8,128)(2,1)S(1)}, f32[192,768]{1,0:T(8,128)S(1)}, f32[192,768]{1,0:T(8,128)S(1)}, f32[192,768]{1,0:T(8,128)S(1)}) custom-call(bf16[256,768]{1,0:T(8,128)(2,1)} %bitcast.25, s32[1,1024]{1,0:T(1,128)} %sources_hbm.1, s32[1,1024]{1,0:T(1,128)} %targets_hbm.1, s32[1,256]{1,0:T(1,128)} %bitcast.27, ...), custom_call_target="tpu_custom_call" | custom-call | tf_op jit(solution)/shard_map/graph_moe/pallas_call | solution.py:410
  100.1 0.7 copy.19
  100.8 0.7 copy.20
  101.6 0.8 copy.21
  102.4 0.8 copy.22
  103.2 0.8 copy.23

commit v3 on v2

--- a/solution.py
+++ b/solution.py
@@ -68,6 +68,14 @@
     following, before = lax.rem(me + 1, EXPERTS), lax.rem(me + EXPERTS - 1, EXPERTS)
     rep_up, rep_down = lax.rem(rep + 1, REPS), lax.rem(rep + REPS - 1, REPS)
 
+    pairs = (
+        (codes_hbm, codes), (d_out_hbm, d_out), (sources_hbm, sources), (targets_hbm, targets),
+        (nodes_hbm, nodes), (gain_hbm, gain), (w_down, wd), (w_gate, wg), (w_up, wu),
+    )
+    loads = [pltpu.make_async_copy(x, y, load_sem.at[i]) for i, (x, y) in enumerate(pairs)]
+    for n in (0, 1, 4):
+        loads[n].start()
+
     barrier = pltpu.get_barrier_semaphore()
 
     def greet(i, carry):
@@ -79,14 +87,8 @@
     lax.fori_loop(1, EXPERTS, greet, 0)
     for z in (rep_up, rep_down):
         pl.semaphore_signal(barrier, inc=1, device_id=(me, z), device_id_type=MESH)
-
-    pairs = (
-        (codes_hbm, codes), (d_out_hbm, d_out), (sources_hbm, sources), (targets_hbm, targets),
-        (nodes_hbm, nodes), (gain_hbm, gain), (w_down, wd), (w_gate, wg), (w_up, wu),
-    )
-    loads = [pltpu.make_async_copy(x, y, load_sem.at[i]) for i, (x, y) in enumerate(pairs)]
-    for load in loads:
-        load.start()
+    for n in (2, 3, 5, 6, 7, 8):
+        loads[n].start()
 
     loads[0].wait()
     code_row = codes[...].astype(F32)
@@ -180,7 +182,7 @@
         dmean[at, :] = (norm * gain_row).astype(BF16)
         return carry
 
-    lax.fori_loop(0, NODES // 32, normalize, 0)
+    lax.fori_loop(0, NODES // 32, normalize, 0, unroll=8)
     bucket(dmean, send_r)
     exchange(send_r, recv_r, 1, 0)
     recv_r[me] = send_r[me]
@@ -246,7 +248,7 @@
                 dup_t[here, :] = (b * silu).astype(BF16)
                 return carry
 
-            lax.fori_loop(0, PART // 16, act, 0)
+            lax.fori_loop(0, PART // 16, act, 0, unroll=6 if i == 0 else 2)
         for j, (left, right) in enumerate(((hid_t, recv_g), (dgate_t, recv_r), (dup_t, recv_r))):
             g = dot(item_rows(i, left), flat(right)).astype(BF16)
             for d in range(2):
@@ -266,7 +268,7 @@
                 ).astype(BF16)
                 return carry
 
-            lax.fori_loop(0, PART // 16, add, 0)
+            lax.fori_loop(0, PART // 16, add, 0, unroll=3)
             hop(d, k, j).start()
 
     exchange_wait(recv_g, 0)
@@ -342,7 +344,7 @@
         total[at, :] = d_out[at, :].astype(F32) + d_mixed
         return carry
 
-    lax.fori_loop(0, NODES // 32, norm_back, 0)
+    lax.fori_loop(0, NODES // 32, norm_back, 0, unroll=4)
     rim_out[...] = dot(counts_t[pl.ds(NODES, 2 * RIM), :], dmean[...]).astype(BF16)
     rim_last = rim_copies(rim_out.at[pl.ds(RIM, RIM)], rim_out.at[pl.ds(0, RIM)], rim_back, 2)
     for copy in rim_last:
@@ -386,10 +388,21 @@
                 )
                 return carry
 
-            lax.fori_loop(0, PART // 16, last, 0)
+            lax.fori_loop(0, PART // 16, last, 0, unroll=6)
     for j in range(3):
         for d in range(2):
             hop(d, 6, j).wait_send()
+
+
+def finish(*refs):
+    count = (len(refs) - 1) // 2
+    copies = [
+        pltpu.make_async_copy(refs[i], refs[count + i], refs[-1].at[i]) for i in range(count)
+    ]
+    for copy in copies:
+        copy.start()
+    for copy in copies:
+        copy.wait()
 
 
 def on_device(node_feats, edge_src, edge_dst, node_codes, norm_gain, w_gate, w_up, w_down_t, d_out):
@@ -455,7 +468,14 @@
         node_feats[0], edge_src, edge_dst, node_codes.reshape(1, NODES), norm_gain,
         w_gate[0], w_up[0], w_down_t[0], d_out[0],
     )
-    layer_out, d_nodes, *grads = out
+    layer_out, d_nodes, *grads = pl.pallas_call(
+        finish,
+        out_shape=outs,
+        in_specs=[pl.BlockSpec(memory_space=vmem)] * 5,
+        out_specs=[hbm] * 5,
+        scratch_shapes=[sem((5,))],
+        name="results",
+    )(*(pltpu.with_memory_space_constraint(x, pltpu.VMEM) for x in out))
     return (layer_out[None], d_nodes[None], *(g.T[None] for g in grads))
 
 

time: 104 us -> 99.4 us (0.956)
  local copies, waits for them, and re-layouts: 3.94 us -> 0 us
    unnamed x5 -> x0, local copies, waits for them, and re-layouts: 3.94 us -> none
    pallas_call x1, Pallas kernels: 99.4 us -> 97 us  [on_device(): pl.pallas_call(kernel, out_shape=[vmem(x.shape, x.dtype) for x in outs],...]
    pallas_call x0 -> x1, Pallas kernels: none -> 1.51 us  [on_device(): pl.pallas_call(finish, out_shape=outs, in_specs=[pl.BlockSpec(memory_spac...]
where the time goes in v3:
time: 99.4 us; the launch traced here: 99.3 us
  Pallas kernels  98.5 us (99%)
    pallas_call x1, Pallas kernels, on_device(): pl.pallas_call(kernel, out_shape=[vmem(x.shape, x.dtype) for x in outs],...  97 us

profile of v3, /device:TPU:1, one launch (start us, length us, event | category | flops | bytes accessed | tf_op | source)
XLA Modules:
  0.0 99.3 jit_solution(14737764611449113537)
XLA Ops:
  0.6 97.0 %graph_moe.1 = (bf16[256,768]{1,0:T(8,128)(2,1)S(1)}, bf16[256,768]{1,0:T(8,128)(2,1)S(1)}, f32[192,768]{1,0:T(8,128)S(1)}, f32[192,768]{1,0:T(8,128)S(1)}, f32[192,768]{1,0:T(8,128)S(1)}) custom-call(bf16[256,768]{1,0:T(8,128)(2,1)} %bitcast.20, s32[1,1024]{1,0:T(1,128)} %sources_hbm.1, s32[1,1024]{1,0:T(1,128)} %targets_hbm.1, s32[1,256]{1,0:T(1,128)} %bitcast.22, ...), custom_call_target="tpu_custom_call" | custom-call | tf_op jit(solution)/shard_map/graph_moe/pallas_call | solution.py:423
  97.7 1.5 %results.1 = (bf16[256,768]{1,0:T(8,128)(2,1)}, bf16[256,768]{1,0:T(8,128)(2,1)}, f32[192,768]{1,0:T(8,128)}, f32[192,768]{1,0:T(8,128)}, f32[192,768]{1,0:T(8,128)}) custom-call(bf16[256,768]{1,0:T(8,128)(2,1)S(1)} %get-tuple-element.15.refs_0_, bf16[256,768]{1,0:T(8,128)(2,1)S(1)} %get-tuple-element.16.refs_1_, f32[192,768]{1,0:T(8,128)S(1)} %get-tuple-element.17.refs_2_, ...), custom_call_target="tpu_custom_call" | custom-call | tf_op jit(solution)/shard_map/results/pallas_call | solution.py:471

commit v4 on v3

--- a/solution.py
+++ b/solution.py
@@ -196,10 +196,6 @@
 
     loads[6].wait()
     turn(wd, wdt)
-    for slot, source in enumerate((send_g, send_r)):
-        exchange_sent(source, slot, 0)
-    exchange(send_g, recv_g, 0, 1)
-    exchange(send_r, recv_r, 1, 1)
     loads[7].wait()
     turn(wg, wgt)
     loads[8].wait()
@@ -271,8 +267,21 @@
             lax.fori_loop(0, PART // 16, add, 0, unroll=3)
             hop(d, k, j).start()
 
-    exchange_wait(recv_g, 0)
-    item_back(0)
+    @pl.when(mc == 0)
+    def _():
+        exchange_wait(recv_g, 0)
+        item_back(0)
+
+    for slot, source in enumerate((send_g, send_r)):
+        exchange_sent(source, slot, 0)
+    exchange(send_g, recv_g, 0, 1)
+    exchange(send_r, recv_r, 1, 1)
+
+    @pl.when(mc == 1)
+    def _():
+        exchange_wait(recv_g, 0)
+        item_back(0)
+
     exchange_wait(recv_r, 1)
     item(0, back=False)
     item(1)

time: 99.4 us -> 97.7 us (0.983)
  Pallas kernels: 98.5 us -> 96.8 us
    pallas_call x1, Pallas kernels: 97 us -> 95.3 us  [on_device(): pl.pallas_call(kernel, out_shape=[vmem(x.shape, x.dtype) for x in outs],...]
where the time goes in v4:
time: 97.7 us; the launch traced here: 97.6 us
  Pallas kernels  96.8 us (99%)
    pallas_call x1, Pallas kernels, on_device(): pl.pallas_call(kernel, out_shape=[vmem(x.shape, x.dtype) for x in outs],...  95.3 us

profile of v4, /device:TPU:1, one launch (start us, length us, event | category | flops | bytes accessed | tf_op | source)
XLA Modules:
  0.0 97.6 jit_solution(2326582220421019007)
XLA Ops:
  0.6 95.3 %graph_moe.1 = (bf16[256,768]{1,0:T(8,128)(2,1)S(1)}, bf16[256,768]{1,0:T(8,128)(2,1)S(1)}, f32[192,768]{1,0:T(8,128)S(1)}, f32[192,768]{1,0:T(8,128)S(1)}, f32[192,768]{1,0:T(8,128)S(1)}) custom-call(bf16[256,768]{1,0:T(8,128)(2,1)} %bitcast.20, s32[1,1024]{1,0:T(1,128)} %sources_hbm.1, s32[1,1024]{1,0:T(1,128)} %targets_hbm.1, s32[1,256]{1,0:T(1,128)} %bitcast.22, ...), custom_call_target="tpu_custom_call" | custom-call | tf_op jit(solution)/shard_map/graph_moe/pallas_call | solution.py:432
  95.9 1.5 %results.1 = (bf16[256,768]{1,0:T(8,128)(2,1)}, bf16[256,768]{1,0:T(8,128)(2,1)}, f32[192,768]{1,0:T(8,128)}, f32[192,768]{1,0:T(8,128)}, f32[192,768]{1,0:T(8,128)}) custom-call(bf16[256,768]{1,0:T(8,128)(2,1)S(1)} %get-tuple-element.15.refs_0_, bf16[256,768]{1,0:T(8,128)(2,1)S(1)} %get-tuple-element.16.refs_1_, f32[192,768]{1,0:T(8,128)S(1)} %get-tuple-element.17.refs_2_, ...), custom_call_target="tpu_custom_call" | custom-call | tf_op jit(solution)/shard_map/results/pallas_call | solution.py:480

commit v5 on v4

--- a/solution.py
+++ b/solution.py
@@ -21,6 +21,7 @@
 REPS = 8
 SLICE = FF // REPS
 PART = SLICE // 2
+EARLY, LATE = 1, 0
 
 
 def partner_order():
@@ -149,7 +150,7 @@
         part = source.at[pl.ds(0, CHIPS)]
         pltpu.make_async_copy(part, part, a2a_send.at[slot, core]).wait()
 
-    exchange(send_g, recv_g, 0, 0)
+    exchange(send_g, recv_g, 0, EARLY)
     recv_g[me] = send_g[me]
 
     loads[2].wait()
@@ -184,7 +185,7 @@
 
     lax.fori_loop(0, NODES // 32, normalize, 0, unroll=8)
     bucket(dmean, send_r)
-    exchange(send_r, recv_r, 1, 0)
+    exchange(send_r, recv_r, 1, EARLY)
     recv_r[me] = send_r[me]
 
     def turn(source, out):
@@ -267,17 +268,17 @@
             lax.fori_loop(0, PART // 16, add, 0, unroll=3)
             hop(d, k, j).start()
 
-    @pl.when(mc == 0)
+    @pl.when(mc == EARLY)
     def _():
         exchange_wait(recv_g, 0)
         item_back(0)
 
     for slot, source in enumerate((send_g, send_r)):
-        exchange_sent(source, slot, 0)
-    exchange(send_g, recv_g, 0, 1)
-    exchange(send_r, recv_r, 1, 1)
-
-    @pl.when(mc == 1)
+        exchange_sent(source, slot, EARLY)
+    exchange(send_g, recv_g, 0, LATE)
+    exchange(send_r, recv_r, 1, LATE)
+
+    @pl.when(mc == LATE)
     def _():
         exchange_wait(recv_g, 0)
         item_back(0)
@@ -377,7 +378,7 @@
         copy.wait_send()
     for slot, source in enumerate((send_g, send_r, back_e, back_d)):
         for core in range(2):
-            if slot > 1 or core == 1:
+            if slot > 1 or core == LATE:
                 exchange_sent(source, slot, core)
         part = source.at[0]
         pltpu.make_async_copy(part, part, a2a_send.at[slot, 2]).wait()

time: 97.7 us -> 97.2 us (level)
  the two profiles are of different devices: /device:TPU:1 before, /device:TPU:4 now
where the time goes in v5:
time: 97.2 us; the launch traced here: 97.1 us
  Pallas kernels  96.3 us (99%)
    pallas_call x1, Pallas kernels, on_device(): pl.pallas_call(kernel, out_shape=[vmem(x.shape, x.dtype) for x in outs],...  94.8 us

profile of v5, /device:TPU:4, one launch (start us, length us, event | category | flops | bytes accessed | tf_op | source)
XLA Modules:
  0.0 97.1 jit_solution(6963246431181597421)
XLA Ops:
  0.6 94.8 %graph_moe.1 = (bf16[256,768]{1,0:T(8,128)(2,1)S(1)}, bf16[256,768]{1,0:T(8,128)(2,1)S(1)}, f32[192,768]{1,0:T(8,128)S(1)}, f32[192,768]{1,0:T(8,128)S(1)}, f32[192,768]{1,0:T(8,128)S(1)}) custom-call(bf16[256,768]{1,0:T(8,128)(2,1)} %bitcast.20, s32[1,1024]{1,0:T(1,128)} %sources_hbm.1, s32[1,1024]{1,0:T(1,128)} %targets_hbm.1, s32[1,256]{1,0:T(1,128)} %bitcast.22, ...), custom_call_target="tpu_custom_call" | custom-call | tf_op jit(solution)/shard_map/graph_moe/pallas_call | solution.py:433
  95.4 1.5 %results.1 = (bf16[256,768]{1,0:T(8,128)(2,1)}, bf16[256,768]{1,0:T(8,128)(2,1)}, f32[192,768]{1,0:T(8,128)}, f32[192,768]{1,0:T(8,128)}, f32[192,768]{1,0:T(8,128)}) custom-call(bf16[256,768]{1,0:T(8,128)(2,1)S(1)} %get-tuple-element.15.refs_0_, bf16[256,768]{1,0:T(8,128)(2,1)S(1)} %get-tuple-element.16.refs_1_, f32[192,768]{1,0:T(8,128)S(1)} %get-tuple-element.17.refs_2_, ...), custom_call_target="tpu_custom_call" | custom-call | tf_op jit(solution)/shard_map/results/pallas_call | solution.py:481

commit v6 on v5

--- a/solution.py
+++ b/solution.py
@@ -22,6 +22,7 @@
 SLICE = FF // REPS
 PART = SLICE // 2
 EARLY, LATE = 1, 0
+GROUP = EXPERTS // 2
 
 
 def partner_order():
@@ -98,16 +99,21 @@
     second = lax.broadcasted_iota(jnp.int32, (NODES, NODES), 1)
     same = code_col == code_row
     rank_row = jnp.sum(jnp.where(same & (first < second), 1.0, 0.0), axis=0, keepdims=True)
-    slot_row = (code_row * CAP + rank_row).astype(jnp.int32)
+    code = codes[...]
+    group = jnp.where(lax.rem(code, 2) == EARLY, 0, ROWS // 2)
+    slot_row = group + lax.div(code, 2) * CAP + rank_row.astype(jnp.int32)
     place_t[...] = jnp.where(
         lax.broadcasted_iota(jnp.int32, (ROWS, NODES), 0) == slot_row, 1.0, 0.0
     ).astype(BF16)
 
-    def bucket(rows, out):
-        out[...] = dot(place_t[...], rows[...]).astype(BF16).reshape(EXPERTS, CAP, D)
+    def bucket(rows, out, core):
+        half = 0 if core == EARLY else 1
+        filled = dot(place_t[pl.ds(half * (ROWS // 2), ROWS // 2), :], rows[...]).astype(BF16)
+        out[pl.ds(half * GROUP, GROUP)] = filled.reshape(GROUP, CAP, D)
 
     loads[1].wait()
-    bucket(d_out, send_g)
+    bucket(d_out, send_g, EARLY)
+    bucket(d_out, send_g, LATE)
     loads[4].wait()
     pl.semaphore_wait(barrier, EXPERTS + 1)
 
@@ -128,19 +134,21 @@
         copy.start()
 
     def exchange(source, landing, slot, core):
-        def send(t, sem):
+        def send(chip, sem):
+            t = chip * 2 + core
+            from_ = t if slot > 1 else chip + (0 if core == EARLY else GROUP)
             pltpu.make_async_remote_copy(
-                source.at[t], landing.at[me], sem, a2a_recv.at[slot],
+                source.at[from_], landing.at[me], sem, a2a_recv.at[slot],
                 device_id=(t, rep), device_id_type=MESH,
             ).start()
 
         for a, b in ORDER:
             chip = lax.rem(my + a, 4) * 4 + lax.rem(mx + b, 4)
-            send(chip * 2 + core, a2a_send.at[slot, core])
+            send(chip, a2a_send.at[slot, core])
 
         @pl.when(mc != core)
         def _():
-            send(my * 8 + mx * 2 + core, a2a_send.at[slot, 2])
+            send(my * 4 + mx, a2a_send.at[slot, 2])
 
     def exchange_wait(landing, slot):
         part = landing.at[pl.ds(0, EXPERTS - 1)]
@@ -151,7 +159,8 @@
         pltpu.make_async_copy(part, part, a2a_send.at[slot, core]).wait()
 
     exchange(send_g, recv_g, 0, EARLY)
-    recv_g[me] = send_g[me]
+    own = jnp.where(mc == EARLY, 0, GROUP) + my * 4 + mx
+    recv_g[me] = send_g[own]
 
     loads[2].wait()
     loads[3].wait()
@@ -184,9 +193,10 @@
         return carry
 
     lax.fori_loop(0, NODES // 32, normalize, 0, unroll=8)
-    bucket(dmean, send_r)
+    bucket(dmean, send_r, EARLY)
     exchange(send_r, recv_r, 1, EARLY)
-    recv_r[me] = send_r[me]
+    bucket(dmean, send_r, LATE)
+    recv_r[me] = send_r[own]
 
     def turn(source, out):
         def body(i, carry):

time: 97.2 us -> 96.9 us (level)
  no operation moved by 1% of the time
where the time goes in v6:
time: 96.9 us; the launch traced here: 96.8 us
  Pallas kernels  96 us (99%)
    pallas_call x1, Pallas kernels, on_device(): pl.pallas_call(kernel, out_shape=[vmem(x.shape, x.dtype) for x in outs],...  94.5 us

profile of v6, /device:TPU:4, one launch (start us, length us, event | category | flops | bytes accessed | tf_op | source)
XLA Modules:
  0.0 96.8 jit_solution(14259615625676987148)
XLA Ops:
  0.6 94.5 %graph_moe.1 = (bf16[256,768]{1,0:T(8,128)(2,1)S(1)}, bf16[256,768]{1,0:T(8,128)(2,1)S(1)}, f32[192,768]{1,0:T(8,128)S(1)}, f32[192,768]{1,0:T(8,128)S(1)}, f32[192,768]{1,0:T(8,128)S(1)}) custom-call(bf16[256,768]{1,0:T(8,128)(2,1)} %bitcast.20, s32[1,1024]{1,0:T(1,128)} %sources_hbm.1, s32[1,1024]{1,0:T(1,128)} %targets_hbm.1, s32[1,256]{1,0:T(1,128)} %bitcast.22, ...), custom_call_target="tpu_custom_call" | custom-call | tf_op jit(solution)/shard_map/graph_moe/pallas_call | solution.py:443
  95.1 1.5 %results.1 = (bf16[256,768]{1,0:T(8,128)(2,1)}, bf16[256,768]{1,0:T(8,128)(2,1)}, f32[192,768]{1,0:T(8,128)}, f32[192,768]{1,0:T(8,128)}, f32[192,768]{1,0:T(8,128)}) custom-call(bf16[256,768]{1,0:T(8,128)(2,1)S(1)} %get-tuple-element.15.refs_0_, bf16[256,768]{1,0:T(8,128)(2,1)S(1)} %get-tuple-element.16.refs_1_, f32[192,768]{1,0:T(8,128)S(1)} %get-tuple-element.17.refs_2_, ...), custom_call_target="tpu_custom_call" | custom-call | tf_op jit(solution)/shard_map/results/pallas_call | solution.py:491

commit v7 on v6

--- a/solution.py
+++ b/solution.py
@@ -296,19 +296,19 @@
     exchange_wait(recv_r, 1)
     item(0, back=False)
     item(1)
+    serve(1, 0)
     item(2)
-    serve(1, 0)
     serve(1, 1)
     item(3)
     serve(1, 2)
+    serve(2, 0)
     item(4)
-    serve(2, 0)
+    serve(2, 1)
     item(5)
-    serve(2, 1)
+    serve(2, 2)
+    serve(3, 0)
     item(6)
-    serve(2, 2)
     item(7)
-    serve(3, 0)
 
     def project(terms, out):
         def body(b, carry):

time: 96.9 us -> 96.9 us (level)
  no operation moved by 1% of the time
where the time goes in v7:
time: 96.9 us; the launch traced here: 96.8 us
  Pallas kernels  96 us (99%)
    pallas_call x1, Pallas kernels, on_device(): pl.pallas_call(kernel, out_shape=[vmem(x.shape, x.dtype) for x in outs],...  94.5 us

profile of v7, /device:TPU:4, one launch (start us, length us, event | category | flops | bytes accessed | tf_op | source)
XLA Modules:
  0.0 96.8 jit_solution(698143189295133800)
XLA Ops:
  0.6 94.5 %graph_moe.1 = (bf16[256,768]{1,0:T(8,128)(2,1)S(1)}, bf16[256,768]{1,0:T(8,128)(2,1)S(1)}, f32[192,768]{1,0:T(8,128)S(1)}, f32[192,768]{1,0:T(8,128)S(1)}, f32[192,768]{1,0:T(8,128)S(1)}) custom-call(bf16[256,768]{1,0:T(8,128)(2,1)} %bitcast.20, s32[1,1024]{1,0:T(1,128)} %sources_hbm.1, s32[1,1024]{1,0:T(1,128)} %targets_hbm.1, s32[1,256]{1,0:T(1,128)} %bitcast.22, ...), custom_call_target="tpu_custom_call" | custom-call | tf_op jit(solution)/shard_map/graph_moe/pallas_call | solution.py:443
  95.1 1.5 %results.1 = (bf16[256,768]{1,0:T(8,128)(2,1)}, bf16[256,768]{1,0:T(8,128)(2,1)}, f32[192,768]{1,0:T(8,128)}, f32[192,768]{1,0:T(8,128)}, f32[192,768]{1,0:T(8,128)}) custom-call(bf16[256,768]{1,0:T(8,128)(2,1)S(1)} %get-tuple-element.15.refs_0_, bf16[256,768]{1,0:T(8,128)(2,1)S(1)} %get-tuple-element.16.refs_1_, f32[192,768]{1,0:T(8,128)S(1)} %get-tuple-element.17.refs_2_, ...), custom_call_target="tpu_custom_call" | custom-call | tf_op jit(solution)/shard_map/results/pallas_call | solution.py:491
